TPU v7x, 512 devices: a whole 4x8x8 slice. The times are simulated.
512 devices in a mesh: dp: 16 (over y, core), rule: 32 (over x, z).
Axes of the slice: x: 4, y: 8, z: 8, core: 2. Of those that a mesh axis runs over, the one named last changes fastest.
Arguments:
- hidden_states: bfloat16 [4096, 8192], P(('dp', 'rule')), may hold values from -6 to 6
- attn_input: bfloat16 [4096, 8192], P(('dp', 'rule')), may hold values from -6 to 6
- rule_ids: int32 [4096, 2], replicated, may hold values from 0 to 127, as said below
- slot_ids: int32 [4096, 2], replicated, may hold values from -1 to 127, as said below
- cotangent: bfloat16 [4096, 2], replicated, may hold values from -6 to 6
- adapter_in: bfloat16 [128, 8192, 512], P('dp', 'rule'), may hold values from -0.0625 to 0.0625
- adapter_bias: float32 [128, 512], P('dp'), may hold values from -3 to 3
- adapter_out: float32 [128, 512], P('dp'), may hold values from -0.25 to 0.25
Outputs:
- rewards: bfloat16 [4096, 2], P('dp')
- adapter_in_grad: bfloat16 [128, 8192, 512], P('dp', 'rule')
- adapter_bias_grad: float32 [128, 512], P('dp')
- adapter_out_grad: float32 [128, 512], P('dp')
- o_proj_grad: bfloat16 [8192, 8192], P('rule', 'dp')
Inputs may be any that keep to these rules, and one draw needn't show every extreme that they name: `rule_ids`: the owner of rule r is r // 8. Among the 16 pairs of one block of 8 consecutive tokens at most 2 name rules of any one owner, and in every block some owner gets exactly 2. The two rules of a token differ. slot_ids[t, k] counts the earlier pairs, in the order of t then k, that name the same rule; it is -1 where that count reaches 128. Some rule fills all 128 rows.
All inputs are finite; a program needn't handle non-finite values.
Results may differ from a plain program's by a relative error of at most 0.03.
Values may be sent and summed in bfloat16 or wider, within the bound.
No kernel may reach another device: no remote copies, remote signals or barrier semaphores. Data moves between devices by JAX's collectives and lax.ppermute only.
A program may use at most 64 MiB of HBM per device.

v0:
```python
import jax
import jax.numpy as jnp
from jax import lax
from jax.sharding import PartitionSpec as P


def local(
    hidden_states, attn_input, rule_ids, slot_ids, cotangent, adapter_in, adapter_bias, adapter_out
):
    dp_size = lax.axis_size("dp")
    rule_size = lax.axis_size("rule")
    dp_index = lax.axis_index("dp")
    rule_index = lax.axis_index("rule")
    rows_dev = hidden_states.shape[0]
    adapters, feature_cols, hidden_units = adapter_in.shape
    send_cap = max(2, 4 * rows_dev // dp_size)
    capacity = 4 * rows_dev * rule_size // adapters
    block_count = dp_size * rule_size
    pair_count = 2 * rows_dev
    slot_count = dp_size * send_cap
    recv_count = slot_count * rule_size
    buffer_rows = adapters * capacity
    rule_all = rule_ids.reshape(block_count, pair_count)
    slot_all = slot_ids.reshape(block_count, pair_count)
    cot_all = cotangent.reshape(block_count, pair_count).astype(jnp.float32)
    owner_all = rule_all // adapters
    earlier = jnp.arange(pair_count)[None, :] < jnp.arange(pair_count)[:, None]
    same_owner = owner_all[:, :, None] == owner_all[:, None, :]
    rank_all = jnp.sum((same_owner & earlier[None]).astype(jnp.int32), axis=2)
    my_block = dp_index * rule_size + rule_index
    my_owner = lax.dynamic_index_in_dim(owner_all, my_block, 0, keepdims=False)
    my_rank = lax.dynamic_index_in_dim(rank_all, my_block, 0, keepdims=False)
    target = my_owner * send_cap + my_rank
    select_pairs = (jnp.arange(slot_count)[:, None] == target[None, :]).astype(jnp.int32)
    select_tokens = jnp.sum(select_pairs.reshape(slot_count, rows_dev, 2), axis=2).astype(
        jnp.bfloat16
    )
    outgoing = jnp.dot(select_tokens, hidden_states, preferred_element_type=jnp.float32).astype(
        jnp.bfloat16
    )
    outgoing = outgoing.reshape(dp_size, send_cap, rule_size, feature_cols)
    incoming = lax.all_to_all(
        lax.all_to_all(outgoing, "dp", split_axis=0, concat_axis=0, tiled=True),
        "rule",
        split_axis=2,
        concat_axis=2,
        tiled=True,
    )
    flat_in = jnp.concatenate(
        [incoming.reshape(recv_count, feature_cols), jnp.zeros((1, feature_cols), jnp.bfloat16)],
        axis=0,
    )
    block_dp = (jnp.arange(block_count) // rule_size)[:, None]
    block_rule = (jnp.arange(block_count) % rule_size)[:, None]
    recv_index = (block_dp * send_cap + rank_all) * rule_size + block_rule
    owned = (owner_all == dp_index) & (slot_all >= 0)
    buffer_pos = rule_all % adapters * capacity + slot_all
    pos_target = jnp.where(owned, buffer_pos, buffer_rows).reshape(-1)
    recv_target = jnp.where(owned, recv_index, recv_count).reshape(-1)
    to_recv = (
        jnp.full((buffer_rows + 1,), recv_count, jnp.int32)
        .at[pos_target]
        .set(recv_index.reshape(-1))[:buffer_rows]
    )
    to_buffer = (
        jnp.full((recv_count + 1,), buffer_rows, jnp.int32)
        .at[recv_target]
        .set(buffer_pos.reshape(-1))[:recv_count]
    )
    cot_buffer = (
        jnp.zeros((buffer_rows + 1,), jnp.float32)
        .at[pos_target]
        .set(cot_all.reshape(-1))[:buffer_rows]
    )
    cot_rows = cot_buffer.reshape(adapters, capacity)
    rows_buf = jnp.take(flat_in, to_recv, axis=0).reshape(adapters, capacity, feature_cols)
    partial_pre = jnp.einsum(
        "acd,adr->acr", rows_buf, adapter_in, preferred_element_type=jnp.float32
    )
    preact = (
        lax.psum(partial_pre.astype(jnp.bfloat16), "rule").astype(jnp.float32)
        + adapter_bias[:, None, :]
    )
    sigmoid_z = jax.nn.sigmoid(preact)
    activated = preact * sigmoid_z
    reward_rows = jnp.sum(activated * adapter_out[:, None, :], axis=2)
    grad_pre = (
        cot_rows[:, :, None]
        * adapter_out[:, None, :]
        * sigmoid_z
        * (1.0 + preact * (1.0 - sigmoid_z))
    )
    grad_half = grad_pre.astype(jnp.bfloat16)
    bias_grad = jnp.sum(grad_pre, axis=1)
    out_grad = jnp.sum(cot_rows[:, :, None] * activated, axis=1)
    reward_flat = jnp.concatenate([reward_rows.reshape(-1), jnp.zeros((1,), jnp.float32)]).astype(
        jnp.bfloat16
    )
    in_grad = jnp.einsum(
        "acd,acr->adr", rows_buf, grad_half, preferred_element_type=jnp.float32
    ).astype(jnp.bfloat16)
    input_grad = jnp.einsum(
        "acr,adr->acd", grad_half, adapter_in, preferred_element_type=jnp.float32
    ).astype(jnp.bfloat16)
    grad_flat = jnp.concatenate(
        [input_grad.reshape(buffer_rows, feature_cols), jnp.zeros((1, feature_cols), jnp.bfloat16)],
        axis=0,
    )
    back_rows = jnp.take(grad_flat, to_buffer, axis=0).reshape(
        dp_size, send_cap, rule_size, feature_cols
    )
    back_reward = jnp.take(reward_flat, to_buffer, axis=0).reshape(dp_size, send_cap, rule_size)
    returned, reward_back = (
        lax.all_to_all(back_rows, "dp", split_axis=0, concat_axis=0, tiled=True),
        lax.all_to_all(back_reward, "dp", split_axis=0, concat_axis=0, tiled=True),
    )
    owner_group = lax.dynamic_slice_in_dim(owner_all, dp_index * rule_size, rule_size, 0)
    rank_group = lax.dynamic_slice_in_dim(rank_all, dp_index * rule_size, rule_size, 0)
    pair_index = (
        (owner_group * send_cap + rank_group) * rule_size + jnp.arange(rule_size)[:, None]
    ).reshape(-1)
    pair_grads = jnp.take(returned.reshape(recv_count, feature_cols), pair_index, axis=0)
    pair_grads = pair_grads.astype(jnp.float32).reshape(rule_size * rows_dev, 2, feature_cols)
    state_grad = jnp.sum(pair_grads, axis=1).astype(jnp.bfloat16)
    rewards = jnp.take(reward_back.reshape(recv_count), pair_index, axis=0).reshape(
        rule_size * rows_dev, 2
    )
    group_term = lax.dot_general(
        state_grad,
        lax.all_gather(attn_input, "rule", axis=0, tiled=True),
        (((0,), (0,)), ((), ())),
        preferred_element_type=jnp.float32,
    )
    o_proj_grad = lax.psum_scatter(
        group_term.astype(jnp.bfloat16), "dp", scatter_dimension=1, tiled=True
    )
    return (rewards, in_grad, bias_grad, out_grad, o_proj_grad)


def solution(mesh):
    placed = (
        P(("dp", "rule"), None),
        P(("dp", "rule"), None),
        P(),
        P(),
        P(),
        P("dp", "rule", None),
        P("dp", None),
        P("dp", None),
    )
    return jax.shard_map(
        local,
        mesh=mesh,
        in_specs=placed,
        out_specs=(
            P("dp", None),
            P("dp", "rule", None),
            P("dp", None),
            P("dp", None),
            P("rule", "dp"),
        ),
        check_vma=False,
    )
```

profile of v0, /device:TPU:25, one launch (start us, length us, event | category | flops | bytes accessed | tf_op | source)
XLA Modules:
  0.0 413.3 jit_solution(5841563843183169320)
XLA Ops:
  7.2 2.9 copy.44
  14.8 9.4 %all-to-all-start = ((bf16[16,2,32,256]{3,1,2,0:T(2,128)(2,1)}), bf16[16,2,32,256]{3,1,2,0:T(2,128)(2,1)S(1)}, u32[]{:S(2)}, u32[]{:S(2)}) async-start(bf16[16,2,32,256]{3,1,2,0:T(2,128)(2,1)} %copy.57), calls=%async_computation | async-start | bytes 1048576 | tf_op jit(solution)/shard_map/all_to_all | solution.py:43
  24.3 3.0 reshape.439
  29.6 3.0 reshape.440
  32.9 6.3 %all-to-all-done = bf16[16,2,32,256]{3,1,2,0:T(2,128)(2,1)S(1)} async-done(((bf16[16,2,32,256]{3,1,2,0:T(2,128)(2,1)}), bf16[16,2,32,256]{3,1,2,0:T(2,128)(2,1)S(1)}, u32[]{:S(2)}, u32[]{:S(2)}) %all-to-all-start) | async-done | bytes 524320 | tf_op jit(solution)/shard_map/all_to_all | solution.py:43
  40.6 11.2 %all-to-all-start.1 = ((bf16[16,2,32,256]{3,1,0,2:T(2,128)(2,1)}), bf16[16,2,32,256]{3,1,0,2:T(2,128)(2,1)S(1)}, u32[]{:S(2)}, u32[]{:S(2)}) async-start(bf16[16,2,32,256]{3,1,0,2:T(2,128)(2,1)} %copy.58), calls=%async_computation.1 | async-start | bytes 1048576 | tf_op jit(solution)/shard_map/all_to_all | solution.py:42
  52.2 30.4 %scatter_custom_fusion.1 = s32[1025]{0:T(1024)S(1)} fusion(s32[8192]{0:T(1024)S(1)} %bitcast.35, s32[8192]{0:T(1024)S(1)} %reshape.505, s32[]{:T(128)} %constant.137.clone.1), kind=kCustom, calls=%fused_computation.76 | custom fusion | bytes 4104 | tf_op jit(solution)/shard_map/scatter | solution.py:63
  83.0 4.9 %gather_fusion.3 = bf16[1024,256]{1,0:T(8,128)(2,1)} fusion(bf16[1025,256]{1,0:T(8,128)(2,1)S(1)} %concatenate.10, s32[1024]{0:T(1024)S(1)} %fusion.23), kind=kCustom, calls=%fused_computation.clone | custom fusion | bytes 1052672 | tf_op jit(solution)/shard_map/jit(_take)/gather | solution.py:76
  91.5 2.7 reshape.441
  94.2 2.7 reshape.442
  97.0 30.4 %scatter_custom_fusion = s32[1025]{0:T(1024)S(1)} fusion(s32[8192]{0:T(1024)S(1)} %bitcast.34, s32[8192]{0:T(1024)S(1)} %fusion.7, s32[]{:T(128)} %constant.137.clone.1), kind=kCustom, calls=%fused_computation.78 | custom fusion | bytes 4104 | tf_op jit(solution)/shard_map/scatter | solution.py:68
  132.0 30.4 %scatter_custom_fusion.2 = f32[1025]{0:T(1024)S(1)} fusion(s32[8192]{0:T(1024)S(1)} %bitcast.36, f32[8192]{0:T(1024)S(1)} %reshape.513, f32[]{:T(128)} %constant.147.clone.1), kind=kCustom, calls=%fused_computation.67 | custom fusion | bytes 4104 | tf_op jit(solution)/shard_map/scatter | solution.py:73
  162.5 83.6 %all-reduce.4.cloned.1.call-done = bf16[8,128,512]{2,1,0:T(8,128)(2,1)} async-done(((bf16[8,128,512]{2,1,0:T(8,128)(2,1)}), bf16[8,128,512]{2,1,0:T(8,128)(2,1)}) %all-reduce.4.cloned.1.call-update) | async-done | bytes 1048592 | tf_op jit(solution)/shard_map/psum | solution.py:81
  246.1 3.4 fusion.29
  249.5 6.8 %gather_fusion = bf16[1024]{0:T(1024)(128)(2,1)S(1)} fusion(bf16[1025]{0:T(1024)(128)(2,1)S(1)} %pad_maximum_fusion, s32[1024]{0:T(1024)S(1)} %get-tuple-element.34), kind=kCustom, calls=%fused_computation.2 | custom fusion | bytes 8192 | tf_op jit(solution)/shard_map/jit(_take)/gather | solution.py:112
  257.0 12.1 %all-to-all-start.2 = ((bf16[16,2,32]{2,1,0:T(2,128)(2,1)}), bf16[16,2,32]{2,1,0:T(2,128)(2,1)S(1)}, u32[]{:S(2)}, u32[]{:S(2)}) async-start(bf16[16,2,32]{2,1,0:T(2,128)(2,1)} %and_select_fusion.2), calls=%async_computation.2 | async-start | bytes 16384 | tf_op jit(solution)/shard_map/all_to_all | solution.py:115
  271.5 5.0 %gather_fusion.4 = bf16[1024,256]{1,0:T(8,128)(2,1)} fusion(bf16[1025,256]{1,0:T(8,128)(2,1)S(1)} %concatenate.12, s32[1024]{0:T(1024)S(1)} %get-tuple-element.34), kind=kCustom, calls=%fused_computation.1.clone | custom fusion | bytes 1052672 | tf_op jit(solution)/shard_map/jit(_take)/gather | solution.py:109
  278.6 7.2 %all-to-all-start.3 = ((bf16[16,2,32,256]{3,2,1,0:T(8,128)(2,1)}), bf16[16,2,32,256]{3,2,1,0:T(8,128)(2,1)S(1)}, u32[]{:S(2)}, u32[]{:S(2)}) async-start(bf16[16,2,32,256]{3,2,1,0:T(8,128)(2,1)} %bitcast.29), calls=%async_computation.3 | async-start | bytes 1048576 | tf_op jit(solution)/shard_map/all_to_all | solution.py:114
  286.5 3.5 gather_fusion.1
  290.3 10.5 %all-to-all-done.3 = bf16[16,2,32,256]{3,2,1,0:T(8,128)(2,1)S(1)} async-done(((bf16[16,2,32,256]{3,2,1,0:T(8,128)(2,1)}), bf16[16,2,32,256]{3,2,1,0:T(8,128)(2,1)S(1)}, u32[]{:S(2)}, u32[]{:S(2)}) %all-to-all-start.3) | async-done | bytes 524320 | tf_op jit(solution)/shard_map/all_to_all | solution.py:114
  304.8 31.3 %all-gather.2.cloned.1.call-done = bf16[256,8192]{1,0:T(8,128)(2,1)} async-done(((bf16[8,8192]{1,0:T(8,128)(2,1)}), bf16[256,8192]{1,0:T(8,128)(2,1)}) %all-gather.2.cloned.1.call-update) | async-done | bytes 4194320 | tf_op jit(solution)/shard_map/all_gather | solution.py:130
  336.2 5.4 %convolution_convert_fusion = bf16[256,8192]{1,0:T(8,128)(2,1)} fusion(bf16[256,256]{1,0:T(8,128)(2,1)S(1)} %fusion.3, bf16[256,8192]{1,0:T(8,128)(2,1)} %all-gather.2.cloned.1.call-done), kind=kOutput, calls=%fused_computation.8 | convolution fusion | flops 1075838976 | bytes 8519680 | tf_op jit(solution)/shard_map/dot_general | solution.py:128
  341.6 3.8 convolution_convert_fusion.2
  346.1 60.7 %reduce-scatter.2.cloned.1.call-done = bf16[256,512]{1,0:T(8,128)(2,1)} async-done(((bf16[256,8192]{1,0:T(8,128)(2,1)}), bf16[256,512]{1,0:T(8,128)(2,1)}) %reduce-scatter.2.cloned.1.call-update) | async-done | bytes 262160 | tf_op jit(solution)/shard_map/reduce_scatter | solution.py:134
  (73 shorter events, 28.0 us)
Async XLA Ops:
  7.2 82.1 %copy-start = (bf16[8,256,512]{2,1,0:T(8,128)(2,1)S(1)}, bf16[8,256,512]{2,1,0:T(8,128)(2,1)}, u32[]{:S(2)}) copy-start(bf16[8,256,512]{2,1,0:T(8,128)(2,1)} %param.15) | copy-start | bytes 6291460
  7.2 5.8 %copy-start.1 = (bf16[8,8192]{1,0:T(8,128)(2,1)S(1)}, bf16[8,8192]{1,0:T(8,128)(2,1)}, u32[]{:S(2)}) copy-start(bf16[8,8192]{1,0:T(8,128)(2,1)} %param.10) | copy-start | bytes 393220
  14.8 12.8 %copy-start.2 = (s32[4096,2]{0,1:T(2,128)S(1)}, s32[4096,2]{0,1:T(2,128)}, u32[]{:S(2)}) copy-start(s32[4096,2]{0,1:T(2,128)} %param.13) | copy-start | bytes 98308
  14.8 24.4 %all-to-all-start = ((bf16[16,2,32,256]{3,1,2,0:T(2,128)(2,1)}), bf16[16,2,32,256]{3,1,2,0:T(2,128)(2,1)S(1)}, u32[]{:S(2)}, u32[]{:S(2)}) async-start(bf16[16,2,32,256]{3,1,2,0:T(2,128)(2,1)} %copy.57), calls=%async_computation | async-start | bytes 1048576 | tf_op jit(solution)/shard_map/all_to_all | solution.py:43
  40.6 42.1 %all-to-all-start.1 = ((bf16[16,2,32,256]{3,1,0,2:T(2,128)(2,1)}), bf16[16,2,32,256]{3,1,0,2:T(2,128)(2,1)S(1)}, u32[]{:S(2)}, u32[]{:S(2)}) async-start(bf16[16,2,32,256]{3,1,0,2:T(2,128)(2,1)} %copy.58), calls=%async_computation.1 | async-start | bytes 1048576 | tf_op jit(solution)/shard_map/all_to_all | solution.py:42
  51.8 194.3 %all-reduce.4.cloned.1.call-start = ((), (), s32[]{:S(2)}) async-start(), calls=%async_computation.5 | async-start | bytes 2097152 | tf_op jit(solution)/shard_map/psum | solution.py:81
  90.7 245.4 %all-gather.2.cloned.1.call-start = ((), (), s32[]{:S(2)}) async-start(), calls=%async_computation.6 | async-start | bytes 4325376 | tf_op jit(solution)/shard_map/all_gather | solution.py:130
  91.5 36.1 %copy-start.3 = (bf16[4096,2]{0,1:T(2,128)(2,1)S(1)}, bf16[4096,2]{0,1:T(2,128)(2,1)}, u32[]{:S(2)}) copy-start(bf16[4096,2]{0,1:T(2,128)(2,1)} %param.14) | copy-start | bytes 49156
  127.5 118.6 %copy-start.4 = (f32[8,512]{1,0:T(8,128)S(1)}, f32[8,512]{1,0:T(8,128)}, u32[]{:S(2)}) copy-start(f32[8,512]{1,0:T(8,128)} %param.16) | copy-start | bytes 49156
  127.5 118.6 %copy-start.5 = (f32[8,512]{1,0:T(8,128)S(1)}, f32[8,512]{1,0:T(8,128)}, u32[]{:S(2)}) copy-start(f32[8,512]{1,0:T(8,128)} %param.17) | copy-start | bytes 49156
  257.0 21.5 %all-to-all-start.2 = ((bf16[16,2,32]{2,1,0:T(2,128)(2,1)}), bf16[16,2,32]{2,1,0:T(2,128)(2,1)S(1)}, u32[]{:S(2)}, u32[]{:S(2)}) async-start(bf16[16,2,32]{2,1,0:T(2,128)(2,1)} %and_select_fusion.2), calls=%async_computation.2 | async-start | bytes 16384 | tf_op jit(solution)/shard_map/all_to_all | solution.py:115
  278.6 22.2 %all-to-all-start.3 = ((bf16[16,2,32,256]{3,2,1,0:T(8,128)(2,1)}), bf16[16,2,32,256]{3,2,1,0:T(8,128)(2,1)S(1)}, u32[]{:S(2)}, u32[]{:S(2)}) async-start(bf16[16,2,32,256]{3,2,1,0:T(8,128)(2,1)} %bitcast.29), calls=%async_computation.3 | async-start | bytes 1048576 | tf_op jit(solution)/shard_map/all_to_all | solution.py:114
  285.8 121.0 %reduce-scatter.2.cloned.1.call-start = ((), (), s32[]{:S(2)}) async-start(), calls=%async_computation.7 | async-start | bytes 4456448 | tf_op jit(solution)/shard_map/reduce_scatter | solution.py:134
Sparse Core Ops, SparseCore 0:
  90.8 155.2 all-reduce.3
  249.3 86.8 all-gather.1
  341.7 65.0 reduce-scatter.1
where the time goes:
time: 414 us; the launch traced here: 413 us
  waiting for transfers between devices  193 us (47%)
  local copies, waits for them, and re-layouts  142 us (34%)
  starting transfers between devices  40.5 us (10%)
  between operations  14.1 us (3%)
  matrix products  13.4 us (3%)
  other arithmetic  10.4 us (3%)
    psum x1, waiting for transfers between devices, local(): lax.psum(partial_pre.astype(jnp.bfloat16), 'rule').astype(jnp.float32)  83.6 us
    reduce_scatter x1, waiting for transfers between devices, local(): lax.psum_scatter(group_term.astype(jnp.bfloat16), 'dp', scatter_dimension...  60.7 us
    all_gather x1, waiting for transfers between devices, local(): lax.all_gather(attn_input, 'rule', axis=0, tiled=True)  31.3 us
    scatter x1, local copies, waits for them, and re-layouts, local(): to_recv = jnp.full((buffer_rows + 1,), recv_count, jnp.int32).at[pos_targ...  30.4 us
    scatter x1, local copies, waits for them, and re-layouts, local(): to_buffer = jnp.full((recv_count + 1,), buffer_rows, jnp.int32).at[recv_t...  30.4 us
    scatter x1, local copies, waits for them, and re-layouts, local(): cot_buffer = jnp.zeros((buffer_rows + 1,), jnp.float32).at[pos_target].se...  30.4 us
    all_to_all x1, starting transfers between devices, local(): lax.all_to_all(back_reward, 'dp', split_axis=0, concat_axis=0, tiled=True)  12.1 us
    all_to_all x1, starting transfers between devices, local(): lax.all_to_all(lax.all_to_all(outgoing, 'dp', split_axis=0, concat_axis=0...  11.2 us
  transfers between devices with their start and end apart: 7, of which 5 were waited for; matrix products, arithmetic and copies ran while one was open for 35% of the time, Pallas kernels for 0%

commit v1 on v0

--- a/solution.py
+++ b/solution.py
@@ -77,8 +77,13 @@
     partial_pre = jnp.einsum(
         "acd,adr->acr", rows_buf, adapter_in, preferred_element_type=jnp.float32
     )
+
+    def list_grid_on(array_here, link_axis):
+        r1 = lax.all_gather(array_here, link_axis)
+        return jnp.sum(r1, axis=0)
+
     preact = (
-        lax.psum(partial_pre.astype(jnp.bfloat16), "rule").astype(jnp.float32)
+        list_grid_on(partial_pre.astype(jnp.bfloat16), "rule").astype(jnp.float32)
         + adapter_bias[:, None, :]
     )
     sigmoid_z = jax.nn.sigmoid(preact)

time: 414 us -> 491 us (1.19)
  waiting for transfers between devices: 193 us -> 267 us
  other arithmetic: 10.4 us -> 19.7 us
    all_gather x0 -> x1, waiting for transfers between devices: none -> 166 us  [list_grid_on(): r1 = lax.all_gather(array_here, link_axis)]
    psum x1 -> x0, waiting for transfers between devices: 83.6 us -> none  [local(): lax.psum(partial_pre.astype(jnp.bfloat16), 'rule').astype(jnp.float32)]
    all_gather x1, waiting for transfers between devices: 31.3 us -> 19.6 us  [local(): lax.all_gather(attn_input, 'rule', axis=0, tiled=True)]
    reduce_sum x0 -> x1, other arithmetic: none -> 11.4 us  [list_grid_on(): return jnp.sum(r1, axis=0)]
  transfers between devices with their start and end apart: 7 -> 7, of which waited for: 5 -> 6; matrix products, arithmetic and copies ran while one was open for 35% -> 31% of each run, Pallas kernels for 0% -> 0%
where the time goes in v1:
time: 491 us; the launch traced here: 490 us
  waiting for transfers between devices  267 us (54%)
  local copies, waits for them, and re-layouts  142 us (29%)
  starting transfers between devices  35.8 us (7%)
  other arithmetic  19.7 us (4%)
  between operations  14.2 us (3%)
  matrix products  11.9 us (2%)
    all_gather x1, waiting for transfers between devices, list_grid_on(): r1 = lax.all_gather(array_here, link_axis)  166 us
    reduce_scatter x1, waiting for transfers between devices, local(): lax.psum_scatter(group_term.astype(jnp.bfloat16), 'dp', scatter_dimension...  59.7 us
    scatter x1, local copies, waits for them, and re-layouts, local(): to_recv = jnp.full((buffer_rows + 1,), recv_count, jnp.int32).at[pos_targ...  30.4 us
    scatter x1, local copies, waits for them, and re-layouts, local(): to_buffer = jnp.full((recv_count + 1,), buffer_rows, jnp.int32).at[recv_t...  30.4 us
    scatter x1, local copies, waits for them, and re-layouts, local(): cot_buffer = jnp.zeros((buffer_rows + 1,), jnp.float32).at[pos_target].se...  30.4 us
    all_gather x1, waiting for transfers between devices, local(): lax.all_gather(attn_input, 'rule', axis=0, tiled=True)  19.6 us
    reduce_sum x1, other arithmetic, list_grid_on(): return jnp.sum(r1, axis=0)  11.4 us
    all_to_all x1, starting transfers between devices, local(): lax.all_to_all(lax.all_to_all(outgoing, 'dp', split_axis=0, concat_axis=0...  11.2 us
  transfers between devices with their start and end apart: 7, of which 6 were waited for; matrix products, arithmetic and copies ran while one was open for 31% of the time, Pallas kernels for 0%

profile of v1, /device:TPU:25, one launch (start us, length us, event | category | flops | bytes accessed | tf_op | source)
XLA Modules:
  0.0 490.1 jit_solution(9637768356110151887)
XLA Ops:
  7.2 2.9 copy.44
  14.8 9.4 %all-to-all-start = ((bf16[16,2,32,256]{3,1,2,0:T(2,128)(2,1)}), bf16[16,2,32,256]{3,1,2,0:T(2,128)(2,1)S(1)}, u32[]{:S(2)}, u32[]{:S(2)}) async-start(bf16[16,2,32,256]{3,1,2,0:T(2,128)(2,1)} %copy.57), calls=%async_computation | async-start | bytes 1048576 | tf_op jit(solution)/shard_map/all_to_all | solution.py:43
  24.3 3.0 reshape.439
  29.6 3.0 reshape.440
  32.9 6.4 %all-to-all-done = bf16[16,2,32,256]{3,1,2,0:T(2,128)(2,1)S(1)} async-done(((bf16[16,2,32,256]{3,1,2,0:T(2,128)(2,1)}), bf16[16,2,32,256]{3,1,2,0:T(2,128)(2,1)S(1)}, u32[]{:S(2)}, u32[]{:S(2)}) %all-to-all-start) | async-done | bytes 524320 | tf_op jit(solution)/shard_map/all_to_all | solution.py:43
  40.6 11.2 %all-to-all-start.1 = ((bf16[16,2,32,256]{3,1,0,2:T(2,128)(2,1)}), bf16[16,2,32,256]{3,1,0,2:T(2,128)(2,1)S(1)}, u32[]{:S(2)}, u32[]{:S(2)}) async-start(bf16[16,2,32,256]{3,1,0,2:T(2,128)(2,1)} %copy.58), calls=%async_computation.1 | async-start | bytes 1048576 | tf_op jit(solution)/shard_map/all_to_all | solution.py:42
  52.2 30.4 %scatter_custom_fusion.1 = s32[1025]{0:T(1024)S(1)} fusion(s32[8192]{0:T(1024)S(1)} %bitcast.33, s32[8192]{0:T(1024)S(1)} %reshape.505, s32[]{:T(128)} %constant.138.clone.1), kind=kCustom, calls=%fused_computation.76 | custom fusion | bytes 4104 | tf_op jit(solution)/shard_map/scatter | solution.py:63
  83.0 3.9 gather_fusion.3
  100.2 30.4 %scatter_custom_fusion = s32[1025]{0:T(1024)S(1)} fusion(s32[8192]{0:T(1024)S(1)} %bitcast.32, s32[8192]{0:T(1024)S(1)} %fusion.7, s32[]{:T(128)} %constant.138.clone.1), kind=kCustom, calls=%fused_computation.78 | custom fusion | bytes 4104 | tf_op jit(solution)/shard_map/scatter | solution.py:68
  130.7 30.4 %scatter_custom_fusion.2 = f32[1025]{0:T(1024)S(1)} fusion(s32[8192]{0:T(1024)S(1)} %bitcast.34, f32[8192]{0:T(1024)S(1)} %reshape.513, f32[]{:T(128)} %constant.148.clone.1), kind=kCustom, calls=%fused_computation.67 | custom fusion | bytes 4104 | tf_op jit(solution)/shard_map/scatter | solution.py:73
  161.2 166.5 %all-gather.6.cloned.1.call-done = bf16[256,128,512]{2,1,0:T(8,128)(2,1)} async-done(((bf16[8,128,512]{2,1,0:T(8,128)(2,1)}), bf16[256,128,512]{2,1,0:T(8,128)(2,1)}) %all-gather.6.cloned.1.call-update) | async-done | bytes 33554448 | tf_op jit(solution)/shard_map/all_gather | solution.py:82
  327.7 11.4 %reduce_sum.71 = bf16[8,128,512]{2,1,0:T(8,128)(2,1)S(1)} reduce(bf16[32,8,128,512]{3,2,1,0:T(8,128)(2,1)} %bitcast.24, bf16[]{:T(256)} %constant.146.clone.1), dimensions={0}, to_apply=%region_4.6 | reduce | flops 16252928 | bytes 34603008 | tf_op jit(solution)/shard_map/reduce_sum | solution.py:83
  340.3 3.9 gather_fusion.4
  344.3 3.4 fusion.29
  347.7 6.8 %gather_fusion = bf16[1024]{0:T(1024)(128)(2,1)S(1)} fusion(bf16[1025]{0:T(1024)(128)(2,1)S(1)} %pad_maximum_fusion, s32[1024]{0:T(1024)S(1)} %get-tuple-element.34), kind=kCustom, calls=%fused_computation.2 | custom fusion | bytes 8192 | tf_op jit(solution)/shard_map/jit(_take)/gather | solution.py:117
  355.2 7.9 %all-to-all-start.2 = ((bf16[16,2,32]{2,1,0:T(2,128)(2,1)}), bf16[16,2,32]{2,1,0:T(2,128)(2,1)S(1)}, u32[]{:S(2)}, u32[]{:S(2)}) async-start(bf16[16,2,32]{2,1,0:T(2,128)(2,1)} %and_select_fusion.2), calls=%async_computation.2 | async-start | bytes 16384 | tf_op jit(solution)/shard_map/all_to_all | solution.py:120
  364.1 3.3 all-to-all-done.2
  367.4 6.7 %all-to-all-start.3 = ((bf16[16,2,32,256]{3,2,1,0:T(8,128)(2,1)}), bf16[16,2,32,256]{3,2,1,0:T(8,128)(2,1)S(1)}, u32[]{:S(2)}, u32[]{:S(2)}) async-start(bf16[16,2,32,256]{3,2,1,0:T(8,128)(2,1)} %bitcast.9), calls=%async_computation.3 | async-start | bytes 1048576 | tf_op jit(solution)/shard_map/all_to_all | solution.py:119
  374.8 3.5 gather_fusion.1
  378.6 10.7 %all-to-all-done.3 = bf16[16,2,32,256]{3,2,1,0:T(8,128)(2,1)S(1)} async-done(((bf16[16,2,32,256]{3,2,1,0:T(8,128)(2,1)}), bf16[16,2,32,256]{3,2,1,0:T(8,128)(2,1)S(1)}, u32[]{:S(2)}, u32[]{:S(2)}) %all-to-all-start.3) | async-done | bytes 524320 | tf_op jit(solution)/shard_map/all_to_all | solution.py:119
  393.4 19.6 %all-gather.4.cloned.1.call-done = bf16[256,8192]{1,0:T(8,128)(2,1)} async-done(((bf16[8,8192]{1,0:T(8,128)(2,1)}), bf16[256,8192]{1,0:T(8,128)(2,1)}) %all-gather.4.cloned.1.call-update) | async-done | bytes 4194320 | tf_op jit(solution)/shard_map/all_gather | solution.py:135
  412.9 5.4 %convolution_convert_fusion = bf16[256,8192]{1,0:T(8,128)(2,1)} fusion(bf16[256,256]{1,0:T(8,128)(2,1)S(1)} %fusion.3, bf16[256,8192]{1,0:T(8,128)(2,1)} %all-gather.4.cloned.1.call-done), kind=kOutput, calls=%fused_computation.8 | convolution fusion | flops 1075838976 | bytes 8519680 | tf_op jit(solution)/shard_map/dot_general | solution.py:133
  419.6 3.6 convolution_convert_fusion.2
  423.8 59.7 %reduce-scatter.2.cloned.1.call-done = bf16[256,512]{1,0:T(8,128)(2,1)} async-done(((bf16[256,8192]{1,0:T(8,128)(2,1)}), bf16[256,512]{1,0:T(8,128)(2,1)}) %reduce-scatter.2.cloned.1.call-update) | async-done | bytes 262160 | tf_op jit(solution)/shard_map/reduce_scatter | solution.py:139
  (80 shorter events, 32.2 us)
Async XLA Ops:
  7.2 80.8 %copy-start = (bf16[8,256,512]{2,1,0:T(8,128)(2,1)S(1)}, bf16[8,256,512]{2,1,0:T(8,128)(2,1)}, u32[]{:S(2)}) copy-start(bf16[8,256,512]{2,1,0:T(8,128)(2,1)} %param.15) | copy-start | bytes 6291460
  7.2 5.8 %copy-start.4 = (bf16[8,8192]{1,0:T(8,128)(2,1)S(1)}, bf16[8,8192]{1,0:T(8,128)(2,1)}, u32[]{:S(2)}) copy-start(bf16[8,8192]{1,0:T(8,128)(2,1)} %param.10) | copy-start | bytes 393220
  14.8 12.8 %copy-start.5 = (s32[4096,2]{0,1:T(2,128)S(1)}, s32[4096,2]{0,1:T(2,128)}, u32[]{:S(2)}) copy-start(s32[4096,2]{0,1:T(2,128)} %param.13) | copy-start | bytes 98308
  14.8 24.4 %all-to-all-start = ((bf16[16,2,32,256]{3,1,2,0:T(2,128)(2,1)}), bf16[16,2,32,256]{3,1,2,0:T(2,128)(2,1)S(1)}, u32[]{:S(2)}, u32[]{:S(2)}) async-start(bf16[16,2,32,256]{3,1,2,0:T(2,128)(2,1)} %copy.57), calls=%async_computation | async-start | bytes 1048576 | tf_op jit(solution)/shard_map/all_to_all | solution.py:43
  40.6 42.1 %all-to-all-start.1 = ((bf16[16,2,32,256]{3,1,0,2:T(2,128)(2,1)}), bf16[16,2,32,256]{3,1,0,2:T(2,128)(2,1)S(1)}, u32[]{:S(2)}, u32[]{:S(2)}) async-start(bf16[16,2,32,256]{3,1,0,2:T(2,128)(2,1)} %copy.58), calls=%async_computation.1 | async-start | bytes 1048576 | tf_op jit(solution)/shard_map/all_to_all | solution.py:42
  51.8 275.9 %all-gather.6.cloned.1.call-start = ((), (), s32[]{:S(2)}) async-start(), calls=%async_computation.7 | async-start | bytes 34603008 | tf_op jit(solution)/shard_map/all_gather | solution.py:82
  87.2 0.8 copy-start.3
  89.4 323.5 %all-gather.4.cloned.1.call-start = ((), (), s32[]{:S(2)}) async-start(), calls=%async_computation.5 | async-start | bytes 4325376 | tf_op jit(solution)/shard_map/all_gather | solution.py:135
  90.2 5.5 %copy-start.6 = (bf16[4096,2]{0,1:T(2,128)(2,1)S(1)}, bf16[4096,2]{0,1:T(2,128)(2,1)}, u32[]{:S(2)}) copy-start(bf16[4096,2]{0,1:T(2,128)(2,1)} %param.14) | copy-start | bytes 49156
  327.7 11.4 %copy-start.7 = (f32[8,512]{1,0:T(8,128)S(1)}, f32[8,512]{1,0:T(8,128)}, u32[]{:S(2)}) copy-start(f32[8,512]{1,0:T(8,128)} %param.16) | copy-start | bytes 49156
  327.7 11.4 %copy-start.8 = (f32[8,512]{1,0:T(8,128)S(1)}, f32[8,512]{1,0:T(8,128)}, u32[]{:S(2)}) copy-start(f32[8,512]{1,0:T(8,128)} %param.17) | copy-start | bytes 49156
  339.2 1.1 copy-start.1
  355.2 12.2 %all-to-all-start.2 = ((bf16[16,2,32]{2,1,0:T(2,128)(2,1)}), bf16[16,2,32]{2,1,0:T(2,128)(2,1)S(1)}, u32[]{:S(2)}, u32[]{:S(2)}) async-start(bf16[16,2,32]{2,1,0:T(2,128)(2,1)} %and_select_fusion.2), calls=%async_computation.2 | async-start | bytes 16384 | tf_op jit(solution)/shard_map/all_to_all | solution.py:120
  367.4 21.9 %all-to-all-start.3 = ((bf16[16,2,32,256]{3,2,1,0:T(8,128)(2,1)}), bf16[16,2,32,256]{3,2,1,0:T(8,128)(2,1)S(1)}, u32[]{:S(2)}, u32[]{:S(2)}) async-start(bf16[16,2,32,256]{3,2,1,0:T(8,128)(2,1)} %bitcast.9), calls=%async_computation.3 | async-start | bytes 1048576 | tf_op jit(solution)/shard_map/all_to_all | solution.py:119
  374.1 109.4 %reduce-scatter.2.cloned.1.call-start = ((), (), s32[]{:S(2)}) async-start(), calls=%async_computation.6 | async-start | bytes 4456448 | tf_op jit(solution)/shard_map/reduce_scatter | solution.py:139
  418.3 1.2 copy-start.2
Sparse Core Ops, SparseCore 0:
  89.6 238.0 all-gather.5
  330.9 82.0 all-gather.3
  418.5 65.0 reduce-scatter.1
